TPU v7x, 32 devices: a whole 2x2x4 slice. The times are simulated.
32 devices in a mesh: param: 8 (over y, x, core), proj: 4 (over z).
Axes of the slice: x: 2, y: 2, z: 4, core: 2. Of those that a mesh axis runs over, the one named last changes fastest.
Arguments:
- query_grads: float32 [256, 65536], P(None, 'param'), may hold values from -45 to 45, as said below
- stored: float32 [8192, 4096], P('param', 'proj'), may hold values from -6 to 6
- proj_seed: int32 [2], replicated, may hold values from 0 to 32748
- offsets: int32 [8], P('param'), may hold values from 0 to 32748
Outputs:
- similarity: float32 [256, 8192], P('proj', 'param')
Inputs may be any that keep to these rules, and one draw needn't show every extreme that they name: `query_grads`: query gradients have row and coordinate scales that differ.
All inputs are finite; a program needn't handle non-finite values.
Results may differ from a plain program's by a relative error of at most 0.0003.
Values sent between devices are 32-bit elements; how exact they have to be, the bound alone decides.
A program may use at most 128 MiB of HBM per device.

v0:
```python
import math

import jax
import jax.numpy as jnp
from jax import lax
from jax.sharding import PartitionSpec as P

modulus = 32749
epsilon = 1e-06


def proj_tile(offset, proj_seed, column_start, coords_count, width_count, param_total, width_total):
    coord_ids = jnp.arange(coords_count, dtype=jnp.int32)[:, None] + offset
    column_ids = column_start + jnp.arange(width_count, dtype=jnp.int32)[None, :]
    coord_hash = (coord_ids * 1103 + proj_seed[0]) % modulus
    column_hash = (column_ids * 2111 + proj_seed[1]) % modulus
    mixed = (coord_hash * column_hash + coord_hash + 3 * column_hash + 17) % modulus
    mixed = (mixed * mixed + coord_hash) % modulus
    uniform_val = (mixed.astype(jnp.float32) + 0.5) * (2.0 / modulus) - 1.0
    column_gain = jnp.sqrt(1.0 + 2.0 * column_ids.astype(jnp.float32) / width_total)
    return uniform_val * column_gain * math.sqrt(3.0 / param_total)


def scores(query_rows, stored):
    return lax.dot_general(
        query_rows,
        stored,
        (((1,), (1,)), ((), ())),
        precision=lax.Precision.HIGHEST,
        preferred_element_type=jnp.float32,
    )


def normalize(query_rows, width_total):
    sum_total = lax.psum(jnp.sum(query_rows * query_rows, axis=1, keepdims=True), "proj")
    return query_rows * lax.rsqrt(sum_total / width_total + epsilon)


def finish(raw_scores, width_total):
    score_scale = 1.0 / math.sqrt(width_total)
    summed = lax.psum_scatter(raw_scores, "proj", scatter_dimension=0, tiled=True)
    return jnp.tanh(summed * score_scale)


def on_device(query_grads, stored, proj_seed, offsets):
    n_param = lax.axis_size("param")
    n_proj = lax.axis_size("proj")
    queries, coords_dev = query_grads.shape
    store_rows, width_dev = stored.shape
    param_total = coords_dev * n_param
    width_total = width_dev * n_proj
    column_start = lax.axis_index("proj") * width_dev
    projection = proj_tile(
        offsets[0], proj_seed, column_start, coords_dev, width_dev, param_total, width_total
    )
    local_part = jnp.dot(
        query_grads, projection, precision=lax.Precision.HIGHEST, preferred_element_type=jnp.float32
    )
    projected = lax.psum(local_part, "param")
    return finish(scores(normalize(projected, width_total), stored), width_total)


def solution(mesh):
    placed = (P(None, "param"), P("param", "proj"), P(), P("param"))
    return jax.shard_map(
        on_device, mesh=mesh, in_specs=placed, out_specs=P("proj", "param"), check_vma=False
    )
```

profile of v0, /device:TPU:0, one launch (start us, length us, event | category | flops | bytes accessed | tf_op | source)
XLA Modules:
  0.0 235.7 jit_solution(15432311417293452482)
XLA Ops:
  6.5 0.0 all-reduce.2.cloned.1.call-start
  7.2 1.3 fusion.48
  8.5 0.6 add_select_fusion.3
  9.1 0.7 add_select_fusion.2
  9.8 110.8 %fusion.29 = f32[256,1024]{0,1:T(8,128)} fusion(f32[256,8192]{1,0:T(8,128)} %param.4, f32[1024]{0:T(1024)S(1)} %add_sqrt_fusion, s32[1024]{0:T(1024)S(1)} %get-tuple-element.8, s32[1024]{0:T(1024)S(1)} %get-tuple-element.7, s32[8192]{0:T(1024)S(1)} %add_select_fusion.2), kind=kOutput, calls=%fused_computation.30 | convolution fusion | flops 25971130368 | bytes 9482240 | tf_op jit(solution)/shard_map/dot_general | solution.py:56
  120.6 0.0 all-reduce.2.cloned.1.call-update
  120.6 0.0 reduce-scatter.2.cloned.1.call-start
  120.7 59.4 %all-reduce.2.cloned.1.call-done = f32[256,1024]{0,1:T(8,128)} async-done(((f32[256,1024]{0,1:T(8,128)}), f32[256,1024]{0,1:T(8,128)}) %all-reduce.2.cloned.1.call-update) | async-done | bytes 1048592 | tf_op jit(solution)/shard_map/psum | solution.py:59
  180.1 1.4 multiply_reduce_fusion
  181.5 11.5 %psum.15 = f32[256,1]{0,1:T(1,128)S(1)} all-reduce(f32[256,1]{0,1:T(1,128)S(1)} %bitcast.12), channel_id=1, replica_groups=mesh['param'=8,'proj'=4] {'proj'}, use_global_device_ids=true, to_apply=%region_2.3 | all-reduce | flops 256 | bytes 2048 | tf_op jit(solution)/shard_map/psum | solution.py:35
  193.0 10.4 %fusion.32 = f32[256,1024]{1,0:T(8,128)} fusion(f32[1024,1024]{1,0:T(8,128)} %param.5, f32[256,1024]{0,1:T(8,128)} %all-reduce.2.cloned.1.call-done, f32[256]{0:T(256)S(1)} %bitcast.13), kind=kOutput, calls=%fused_computation.31 | convolution fusion | flops 3221487616 | bytes 6292480 | tf_op jit(solution)/shard_map/dot_general | solution.py:25
  203.4 0.0 reduce-scatter.2.cloned.1.call-update
  203.4 23.7 %reduce-scatter.2.cloned.1.call-done = f32[64,1024]{1,0:T(8,128)} async-done(((f32[256,1024]{1,0:T(8,128)}), f32[64,1024]{1,0:T(8,128)}) %reduce-scatter.2.cloned.1.call-update) | async-done | bytes 262160 | tf_op jit(solution)/shard_map/reduce_scatter | solution.py:41
  227.2 1.7 multiply_tanh_fusion
  (2 shorter events, 0.0 us)
Async XLA Ops:
  6.5 173.6 %all-reduce.2.cloned.1.call-start = ((), (), s32[]{:S(2)}) async-start(), calls=%async_computation.1 | async-start | bytes 2097152 | tf_op jit(solution)/shard_map/psum | solution.py:59
  120.6 106.5 %reduce-scatter.2.cloned.1.call-start = ((), (), s32[]{:S(2)}) async-start(), calls=%async_computation.2 | async-start | bytes 1310720 | tf_op jit(solution)/shard_map/reduce_scatter | solution.py:41
Sparse Core Ops, SparseCore 0:
  120.8 59.2 all-reduce.1
  203.5 23.5 reduce-scatter.1
where the time goes:
time: 236 us
  matrix products  121 us (51%)
  waiting for transfers between devices  83.2 us (35%)
  between operations  14.1 us (6%)
  blocking collectives  11.5 us (5%)
  other arithmetic  4.35 us (2%)
    dot_general x1, matrix products, on_device(): jnp.dot(query_grads, projection, precision=lax.Precision.HIGHEST, preferr...  111 us
    psum x1, waiting for transfers between devices, on_device(): projected = lax.psum(local_part, 'param')  59.4 us
    reduce_scatter x1, waiting for transfers between devices, finish(): lax.psum_scatter(raw_scores, 'proj', scatter_dimension=0, tiled=True)  23.7 us
    psum x1, blocking collectives, normalize(): lax.psum(jnp.sum(query_rows * query_rows, axis=1, keepdims=True), 'proj')  11.5 us
    dot_general x1, matrix products, scores(): lax.dot_general(query_rows, stored, (((1,), (1,)), ((), ())), precision=l...  10.4 us
  transfers between devices with their start and end apart: 2, of which 2 were waited for; matrix products, arithmetic and copies ran while one was open for 0% of the time, Pallas kernels for 0%

commit v1 on v0

v1 whole, which is shorter than its diff:
```python
import functools
import math

import jax
import jax.numpy as jnp
import numpy as np
from jax import lax
from jax.experimental import pallas as pl
from jax.experimental.pallas import tpu as pltpu
from jax.sharding import PartitionSpec as P

modulus = 32749
middle = modulus // 2
epsilon = 1e-06
bits = 8
block = 1 << bits
pairs = [(p, q) for p in range(bits) for q in range(p + 1, bits)]
pair_rows = 64
vary_rows = 32
slab_blocks = 4


def centred(value):
    value = value % modulus
    return jnp.where(value > middle, value - modulus, value)


def two_pieces(value):
    low = ((value + 64) & 127) - 64
    return (value - low).astype(jnp.bfloat16), low.astype(jnp.bfloat16)


def bit_features():
    digits = (np.arange(block)[:, None] >> np.arange(bits)[None, :]) & 1
    cross = np.stack([digits[:, p] * digits[:, q] for p, q in pairs], axis=1)
    vary = np.concatenate([digits, np.ones((block, 1), digits.dtype)], axis=1)
    out = np.zeros((block, 128), np.float32)
    out[:, : len(pairs)] = cross
    out[:, len(pairs) : 2 * len(pairs)] = cross
    out[:, pair_rows : pair_rows + bits + 1] = vary
    out[:, pair_rows + bits + 1 : pair_rows + 2 * (bits + 1)] = vary
    return jnp.asarray(out, jnp.bfloat16)


def coefficients(offset, proj_seed, column_start, coords, width):
    column = column_start + jnp.arange(width, dtype=jnp.int32)[None, :]
    start = (offset * 1103 + proj_seed[0]) % modulus
    factor = ((column * 2111 + proj_seed[1]) % modulus) + 1
    slope = (factor * 1103) % modulus
    level = ((start + 3) * factor + 14) % modulus
    square = (slope * slope) % modulus
    linear = ((slope * level) % modulus * 2 + 1103) % modulus
    constant = (level * level + start) % modulus
    base = ((jnp.arange(coords // block, dtype=jnp.int32) * block) % modulus)[:, None]
    linear_at = (linear + (square * base) % modulus * 2) % modulus
    constant_at = (((square * base) % modulus + linear) % modulus * base + constant) % modulus
    cross = centred(
        jnp.concatenate([(square * (2 ** (p + q + 1))) % modulus for p, q in pairs], axis=0)
    )
    vary = [centred((square * 4**p) % modulus + linear_at * 2**p) for p in range(bits)]
    vary.append(centred(constant_at - middle))
    vary = jnp.stack(vary, axis=1)
    cross_high, cross_low = two_pieces(cross)
    vary_high, vary_low = two_pieces(vary)
    cross = jnp.concatenate([cross_high, cross_low], axis=0)
    cross = jnp.pad(cross, ((0, pair_rows - cross.shape[0]), (0, 0)))
    vary = jnp.concatenate([vary_high, vary_low], axis=1)
    vary = jnp.pad(vary, ((0, 0), (0, vary_rows - vary.shape[1]), (0, 0)))
    return cross, vary


def project_kernel(chunk, feat_ref, cross_ref, vary_ref, gain_ref, grads_ref, out_ref,
                   stage, high_q, low_q, high_a, low_a, high_b, low_b, total, sems):
    queries, coords = high_q.shape
    width = out_ref.shape[1]
    slab = block * slab_blocks
    slabs = coords // slab

    def fetch(s):
        return pltpu.make_async_copy(
            grads_ref.at[:, pl.ds(pl.multiple_of(s * slab, slab), slab)], stage.at[s], sems.at[s]
        )

    def make(s, column, high, low):
        cross = cross_ref[:, pl.ds(column, chunk)]
        blank = jnp.zeros((128 - pair_rows - vary_rows, chunk), jnp.bfloat16)
        for part in range(slab_blocks):
            vary = vary_ref[s * slab_blocks + part, :, pl.ds(column, chunk)]
            coef = jnp.concatenate([cross, vary, blank], axis=0)
            x = jnp.dot(feat_ref[...], coef, preferred_element_type=jnp.float32)
            x = x * (1.0 / modulus)
            x = x - jnp.round(x)
            top = x.astype(jnp.bfloat16)
            high[pl.ds(part * block, block), :] = top
            low[pl.ds(part * block, block), :] = (x - top.astype(jnp.float32)).astype(jnp.bfloat16)

    def use(s, high, low):
        at = pl.ds(pl.multiple_of(s * slab, slab), slab)
        qh = high_q[:, at]
        ql = low_q[:, at]
        wh = high[...]
        wl = low[...]
        total[...] += (
            jnp.dot(qh, wh, preferred_element_type=jnp.float32)
            + jnp.dot(ql, wh, preferred_element_type=jnp.float32)
            + jnp.dot(qh, wl, preferred_element_type=jnp.float32)
        )

    for s in range(slabs):
        fetch(s).start()

    @pl.loop(0, slabs)
    def _(s):
        fetch(s).wait()
        at = pl.ds(pl.multiple_of(s * slab, slab), slab)
        q = stage[s]
        top = q.astype(jnp.bfloat16)
        high_q[:, at] = top
        low_q[:, at] = (q - top.astype(jnp.float32)).astype(jnp.bfloat16)

    @pl.loop(0, width // chunk)
    def _(n):
        column = pl.multiple_of(n * chunk, chunk)
        total[...] = jnp.zeros_like(total)
        make(0, column, high_a, low_a)

        @pl.loop(0, slabs // 2)
        def _(pair):
            s = pair * 2
            make(s + 1, column, high_b, low_b)
            use(s, high_a, low_a)
            make(lax.rem(s + 2, slabs), column, high_a, low_a)
            use(s + 1, high_b, low_b)

        out_ref[:, pl.ds(column, chunk)] = total[...] * gain_ref[:, pl.ds(column, chunk)]


def project(query_grads, cross, vary, gain):
    queries, coords = query_grads.shape
    width = gain.shape[1]
    chunk = 256
    slab = block * slab_blocks
    vmem = pl.BlockSpec(memory_space=pltpu.VMEM)
    half = pltpu.VMEM((slab, chunk), jnp.bfloat16)
    return pl.pallas_call(
        functools.partial(project_kernel, chunk),
        out_shape=jax.ShapeDtypeStruct((queries, width), jnp.float32),
        in_specs=[vmem] * 4 + [pl.BlockSpec(memory_space=pl.ANY)],
        out_specs=vmem,
        scratch_shapes=[
            pltpu.VMEM((coords // slab, queries, slab), jnp.float32),
            pltpu.VMEM((queries, coords), jnp.bfloat16),
            pltpu.VMEM((queries, coords), jnp.bfloat16),
            half, half, half, half,
            pltpu.VMEM((queries, chunk), jnp.float32),
            pltpu.SemaphoreType.DMA((coords // slab,)),
        ],
        compiler_params=pltpu.CompilerParams(vmem_limit_bytes=48 * 1024 * 1024),
        name="project",
    )(bit_features(), cross, vary, gain, query_grads)


def on_device(query_grads, stored, proj_seed, offsets):
    n_param = lax.axis_size("param")
    n_proj = lax.axis_size("proj")
    queries, coords = query_grads.shape
    store_rows, width = stored.shape
    param_total = coords * n_param
    width_total = width * n_proj
    column_start = lax.axis_index("proj") * width
    cross, vary = coefficients(offsets[0], proj_seed, column_start, coords, width)
    column = (column_start + jnp.arange(width, dtype=jnp.int32)[None, :]).astype(jnp.float32)
    gain = jnp.sqrt(1.0 + 2.0 * column / width_total) * (2.0 * math.sqrt(3.0 / param_total))
    local = project(query_grads, cross, vary, gain)
    projected = lax.psum(local, "param")
    raw = lax.dot_general(
        projected, stored, (((1,), (1,)), ((), ())),
        precision=lax.Precision.HIGH, preferred_element_type=jnp.float32,
    )
    squares = jnp.sum(projected * projected, axis=1, keepdims=True)
    squares = lax.psum_scatter(squares, "proj", scatter_dimension=0, tiled=True)
    inverse = lax.rsqrt(squares / width_total + epsilon)
    summed = lax.psum_scatter(raw, "proj", scatter_dimension=0, tiled=True)
    return jnp.tanh(summed * (inverse * (1.0 / math.sqrt(width_total))))


def solution(mesh):
    placed = (P(None, "param"), P("param", "proj"), P(), P("param"))
    return jax.shard_map(
        on_device, mesh=mesh, in_specs=placed, out_specs=P("proj", "param"), check_vma=False
    )
```

time: 236 us -> 177 us (0.75)
  matrix products: 121 us -> 5.42 us
  Pallas kernels: 0 us -> 26.2 us
  other arithmetic: 4.35 us -> 26.9 us
  waiting for transfers between devices: 83.2 us -> 99.2 us
  blocking collectives: 11.5 us -> 0 us
  local copies, waits for them, and re-layouts: 1.31 us -> 4.32 us
    dot_general x2 -> x1, matrix products: 121 us -> 5.42 us  [on_device(): lax.dot_general(projected, stored, (((1,), (1,)), ((), ())), precision=la...]
    pallas_call x0 -> x1, Pallas kernels: none -> 26.2 us  [project(): pl.pallas_call(functools.partial(project_kernel, chunk), out_shape=jax.Sh...]
    select_n x2 -> x16, other arithmetic: 1.26 us -> 19.5 us  [the longest x2 10.1 us: centred(): return jnp.where(value > middle, value - modulus, value)]
    unnamed x2 -> x4, waiting for transfers between devices: 0.03 us -> 13 us
    psum x1 -> x0, blocking collectives: 11.5 us -> none  [normalize(): lax.psum(jnp.sum(query_rows * query_rows, axis=1, keepdims=True), 'proj')]
    reduce_scatter x1, waiting for transfers between devices: 23.7 us -> 26.8 us  [on_device(): summed = lax.psum_scatter(raw, 'proj', scatter_dimension=0, tiled=True)]
  transfers between devices with their start and end apart: 2 -> 3, of which waited for: 2 -> 3; matrix products, arithmetic and copies ran while one was open for 0% -> 4% of each run, Pallas kernels for 0% -> 0%
where the time goes in v1:
time: 177 us
  waiting for transfers between devices  99.2 us (56%)
  other arithmetic  26.9 us (15%)
  Pallas kernels  26.2 us (15%)
  between operations  14.5 us (8%)
  matrix products  5.42 us (3%)
  local copies, waits for them, and re-layouts  4.32 us (2%)
    psum x1, waiting for transfers between devices, on_device(): projected = lax.psum(local, 'param')  59.4 us
    reduce_scatter x1, waiting for transfers between devices, on_device(): summed = lax.psum_scatter(raw, 'proj', scatter_dimension=0, tiled=True)  26.8 us
    pallas_call x1, Pallas kernels, project(): pl.pallas_call(functools.partial(project_kernel, chunk), out_shape=jax.Sh...  26.2 us
    unnamed x4, waiting for transfers between devices  13 us
    select_n x2, other arithmetic, centred(): return jnp.where(value > middle, value - modulus, value)  10.1 us
    select_n x10, other arithmetic, coefficients(): square * 2 ** (p + q + 1) % modulus  7.35 us
    dot_general x1, matrix products, on_device(): lax.dot_general(projected, stored, (((1,), (1,)), ((), ())), precision=la...  5.42 us
  transfers between devices with their start and end apart: 3, of which 3 were waited for; matrix products, arithmetic and copies ran while one was open for 4% of the time, Pallas kernels for 0%

profile of v1, /device:TPU:0, one launch (start us, length us, event | category | flops | bytes accessed | tf_op | source)
XLA Modules:
  0.0 176.7 jit_solution(8553647209835213521)
XLA Ops:
  6.5 0.0 all-reduce.4.cloned.1.call-start
  6.5 1.3 fusion.25
  9.2 0.7 add_select_fusion.1
  9.9 0.7 add_select_fusion.9
  10.6 0.7 add_select_fusion.13
  11.3 0.7 add_select_fusion.3
  12.0 0.7 add_select_fusion.5
  12.6 0.7 add_select_fusion.7
  13.3 0.8 and_select_fusion.13
  14.1 0.8 and_select_fusion.15
  14.9 0.8 and_select_fusion.17
  15.6 0.8 and_select_fusion.19
  16.4 0.8 and_select_fusion.21
  17.1 0.8 and_select_fusion.23
  17.9 0.7 and_select_fusion.25
  18.7 4.6 %compare_select_fusion.1 = (s32[32,1,1024]{2,1,0:T(1,128)S(1)}, s32[32,1,1024]{2,1,0:T(1,128)S(1)}, s32[32,1,1024]{2,1,0:T(1,128)S(1)}) fusion(s32[1024]{0:T(1024)S(1)} %get-tuple-element.34, s32[32]{0:T(128)S(1)} %and_select_fusion.29, s32[1024]{0:T(1024)S(1)} %add_select_fusion.13, s32[1024]{0:T(1024)S(1)} %get-tuple-element.41, s32[1024]{0:T(1024)S(1)} %get-tuple-element.33), kind=kLoop, calls=%fused_computation.9 | loop fusion | flops 1671168 | bytes 409728 | tf_op jit(solution)/shard_map/jit(_where)/select_n | solution.py:25
  23.2 5.6 %compare_select_fusion.2 = (s32[32,1,1024]{2,1,0:T(1,128)S(1)}, s32[32,1,1024]{2,1,0:T(1,128)S(1)}, s32[32,1,1024]{2,1,0:T(1,128)S(1)}, s32[32,1,1024]{2,1,0:T(1...) fusion(s32[32,1,1024]{2,1,0:T(1,128)S(1)} %get-tuple-element.6, ...), kind=kLoop, calls=%fused_computation.10 | loop fusion | flops 2490368 | bytes 1077248 | tf_op jit(solution)/shard_map/jit(_where)/select_n | solution.py:25
  28.8 1.9 %stack.2 = s32[32,9,1024]{2,1,0:T(8,128)S(1)} concatenate(s32[32,1,1024]{2,1,0:T(1,128)S(1)} %get-tuple-element.15, s32[32,1,1024]{2,1,0:T(1,128)S(1)} %get-tuple-element.14, s32[32,1,1024]{2,1,0:T(1,128)S(1)} %get-tuple-element.13, s32[32,1,1024]{2,1,0:T(1,128)S(1)} %get-tuple-element.12, s32[32,1,1024]{2,1,0:T(1,128)S(1)} %get-tuple-element.11, ...), dimensions={1} | concatenate | bytes 2359296 | tf_op jit(solution)/shard_map/stack | solution.py:62
  30.7 1.5 subtract_convert_fusion
  32.2 0.2 concatenate.9
  32.4 0.1 subtract_convert_fusion.1
  32.5 0.0 copy-start
  32.6 1.8 %fusion.2.vary_ref = bf16[32,32,1024]{2,1,0:T(8,128)(2,1)S(1)} fusion(bf16[32,9,1024]{2,1,0:T(8,128)(2,1)} %get-tuple-element.8, bf16[32,9,1024]{2,1,0:T(8,128)(2,1)S(1)} %get-tuple-element.7), kind=kLoop, calls=%fused_computation.3 | loop fusion | flops 7340032 | bytes 3276800 | tf_op jit(solution)/shard_map/concatenate | solution.py:67
  34.4 0.0 copy-done
  34.4 26.2 %project.1 = f32[256,1024]{1,0:T(8,128)} custom-call(bf16[256,128]{1,0:T(8,128)(2,1)S(1)} %copy-done, bf16[64,1024]{1,0:T(8,128)(2,1)S(1)} %fusion.6.cross_ref, bf16[32,32,1024]{2,1,0:T(8,128)(2,1)S(1)} %fusion.2.vary_ref, f32[1,1024]{1,0:T(1,128)S(1)} %sqrt_multiply_fusion.gain_ref, f32[256,8192]{1,0:T(8,128)} %grads_ref.1), custom_call_target="tpu_custom_call" | custom-call | tf_op jit(solution)/shard_map/project/pallas_call | solution.py:145
  60.7 0.0 all-reduce.4.cloned.1.call-update
  60.7 0.0 reduce-scatter.7.cloned.1.call-start
  60.7 59.4 %all-reduce.4.cloned.1.call-done = f32[256,1024]{1,0:T(8,128)} async-done(((f32[256,1024]{1,0:T(8,128)}), f32[256,1024]{1,0:T(8,128)}) %all-reduce.4.cloned.1.call-update) | async-done | bytes 1048592 | tf_op jit(solution)/shard_map/psum | solution.py:175
  120.1 1.4 multiply_reduce_fusion
  121.5 0.8 copy.6
  122.3 0.0 reduce-scatter.7.cloned.1.call-update
  122.3 0.0 reduce-scatter.5.cloned.1.call-start
  122.4 5.4 %fusion.26 = f32[256,1024]{1,0:T(8,128)} fusion(f32[256,1024]{1,0:T(8,128)} %all-reduce.4.cloned.1.call-done, f32[1024,1024]{1,0:T(8,128)} %param.6), kind=kOutput, calls=%fused_computation.106 | convolution fusion | flops 1610612736 | bytes 6291456 | tf_op jit(solution)/shard_map/dot_general | solution.py:176
  127.8 0.0 reduce-scatter.5.cloned.1.call-update
  127.8 12.9 %reduce-scatter.7.cloned.1.call-done = f32[64,1]{1,0:T(8,128)} async-done(((f32[256,1]{1,0:T(8,128)}), f32[64,1]{1,0:T(8,128)}) %reduce-scatter.7.cloned.1.call-update) | async-done | bytes 272
  140.7 0.8 rsqrt_multiply_fusion
  141.5 0.1 copy.8
  141.6 26.8 %reduce-scatter.5.cloned.1.call-done = f32[64,1024]{1,0:T(8,128)} async-done(((f32[256,1024]{1,0:T(8,128)}), f32[64,1024]{1,0:T(8,128)}) %reduce-scatter.5.cloned.1.call-update) | async-done | bytes 262160 | tf_op jit(solution)/shard_map/reduce_scatter | solution.py:183
  168.4 1.8 multiply_tanh_fusion
  (3 shorter events, 0.1 us)
Async XLA Ops:
  6.5 113.6 %all-reduce.4.cloned.1.call-start = ((), (), s32[]{:S(2)}) async-start(), calls=%async_computation.2 | async-start | bytes 2097152 | tf_op jit(solution)/shard_map/psum | solution.py:175
  32.5 1.9 %copy-start = (bf16[256,128]{1,0:T(8,128)(2,1)S(1)}, bf16[256,128]{1,0:T(8,128)(2,1)}, u32[]{:S(2)}) copy-start(bf16[256,128]{1,0:T(8,128)(2,1)} %constant.304.clone.feat_ref) | copy-start | bytes 196612
  60.7 80.0 %reduce-scatter.7.cloned.1.call-start = ((), (), s32[]{:S(2)}) async-start(), calls=%async_computation.4 | async-start | bytes 163840
  122.3 46.1 %reduce-scatter.5.cloned.1.call-start = ((), (), s32[]{:S(2)}) async-start(), calls=%async_computation.3 | async-start | bytes 1310720 | tf_op jit(solution)/shard_map/reduce_scatter | solution.py:183
Sparse Core Ops, SparseCore 0:
  60.8 59.2 all-reduce.3
  122.5 18.2 reduce-scatter.6
  143.1 25.2 reduce-scatter.4

commit v2 on v0

v2 whole, which is shorter than its diff:
```python
import functools
import math

import jax
import jax.numpy as jnp
import numpy as np
from jax import lax
from jax.experimental import pallas as pl
from jax.experimental.pallas import tpu as pltpu
from jax.sharding import PartitionSpec as P

modulus = 32749
middle = modulus // 2
epsilon = 1e-06
bits = 8
block = 1 << bits
pairs = [(p, q) for p in range(bits) for q in range(p + 1, bits)]
slab_blocks = 4
slab = block * slab_blocks
chunk = 256
pieces = 2
MESH = pl.DeviceIdType.MESH


def bit_features():
    digits = (np.arange(block)[:, None] >> np.arange(bits)[None, :]) & 1
    cross = np.stack([digits[:, p] * digits[:, q] for p, q in pairs], axis=1)
    vary = np.concatenate([digits, np.ones((block, 1), digits.dtype)], axis=1)
    out = np.zeros((block, 128), np.float32)
    for at in (0, 32):
        out[:, at : at + len(pairs)] = cross
    for at in (64, 80):
        out[:, at : at + bits + 1] = vary
    return jnp.asarray(out, jnp.bfloat16)


def pair_weights():
    out = np.zeros((32, 128), np.int32)
    for row, (p, q) in enumerate(pairs):
        out[row] = 2 ** (p + q + 1)
    return jnp.asarray(out)


def reduced(value):
    times = jnp.round(value.astype(jnp.float32) * (1.0 / modulus)).astype(jnp.int32)
    return value - times * modulus


def reduced_float(value):
    return value - jnp.round(value * (1.0 / modulus)) * modulus


def two_pieces(value):
    high = jnp.round(value * (1.0 / 128)) * 128.0
    return high.astype(jnp.bfloat16), (value - high).astype(jnp.bfloat16)


def split(value):
    high = value.astype(jnp.bfloat16)
    return high, (value - high.astype(jnp.float32)).astype(jnp.bfloat16)


def mix(a, b):
    return jnp.dot(a, b, preferred_element_type=jnp.float32)


def mix_rows(a, b):
    return lax.dot_general(a, b, (((1,), (1,)), ((), ())), preferred_element_type=jnp.float32)


def kernel(n_param, n_proj, offset_ref, seed_ref, feat_ref, weight_ref, grads_ref, stored_ref, out_ref,
           stage, store, high_q, low_q, cross, vary, high_a, low_a, high_b, low_b, total,
           part, pair_in, ring_in, proj, raw, square_out, square_in, column_sum, line_in,
           grad_sem, store_sem, pair_sem, ring_sem, gather_sem, back_sem, square_sem, line_sem):
    queries, coords = high_q.shape
    store_rows, width = store.shape
    slabs = coords // slab
    chunks = width // chunk
    chips = n_param // 2
    half = queries // 2
    own = half // chips
    share = queries // n_proj
    piece = share // pieces
    me = lax.axis_index("param")
    here = lax.axis_index("proj")
    core = lax.rem(me, 2)
    chip = lax.div(me, 2)
    sibling = me + 1 - 2 * core
    width_total = width * n_proj
    scale = 2.0 * math.sqrt(3.0 / (coords * n_param))

    def partner(o):
        return lax.rem(chip + o, chips)

    def fetch(s):
        return pltpu.make_async_copy(
            grads_ref.at[:, pl.ds(pl.multiple_of(s * slab, slab), slab)], stage.at[s], grad_sem.at[s]
        )

    for s in range(slabs):
        fetch(s).start()
    fetch_store = pltpu.make_async_copy(stored_ref, store, store_sem)
    fetch_store.start()

    barrier = pltpu.get_barrier_semaphore()
    pl.semaphore_signal(barrier, inc=1, device_id={"param": sibling}, device_id_type=MESH)
    for o in range(1, chips):
        pl.semaphore_signal(
            barrier, inc=1, device_id={"param": partner(o) * 2 + core}, device_id_type=MESH
        )
    for o in range(1, n_proj):
        pl.semaphore_signal(
            barrier, inc=1, device_id={"proj": lax.rem(here + o, n_proj)}, device_id_type=MESH
        )

    for n in range(chunks):
        at = pl.ds(n * chunk, chunk)
        shape = (16, chunk)
        column = here * width + n * chunk + lax.broadcasted_iota(jnp.int32, shape, 1)
        row = lax.broadcasted_iota(jnp.int32, shape, 0)
        start = reduced(jnp.full(shape, offset_ref[0] * 1103 + seed_ref[0], jnp.int32))
        factor = reduced(column * 2111 + seed_ref[1]) + 1
        slope = reduced(factor * 1103)
        level = reduced((start + 3) * factor + 14)
        square = reduced(slope * slope)
        linear = reduced(reduced(slope * level) * 2 + 1103)
        constant = reduced(level * level + start)
        weights = jnp.concatenate([weight_ref[...]] * (chunk // 128), axis=1)
        pair_coef = reduced(jnp.concatenate([square, square], axis=0) * weights)
        high, low = two_pieces(pair_coef.astype(jnp.float32))
        cross[pl.ds(0, 32), at] = high
        cross[pl.ds(32, 32), at] = low
        power = jnp.where(row < bits, jnp.left_shift(1, jnp.minimum(row, bits)), 0)
        first = reduced(reduced(square * power) * power + linear * power)
        first = jnp.where(row == bits, reduced(constant - middle), first)
        twice = reduced(square * (2 * block))
        step = reduced(twice * power)
        leap = reduced(reduced(square * block) * block + linear * block)
        step = jnp.where(row == bits, leap, step)
        bend = jnp.where(row == bits, reduced(twice * block), 0)
        bend = bend.astype(jnp.float32)

        def advance(i, state):
            value, step = state
            high, low = two_pieces(value)
            vary[i, pl.ds(0, 16), at] = high
            vary[i, pl.ds(16, 16), at] = low
            return reduced_float(value + step), reduced_float(step + bend)

        lax.fori_loop(
            0, coords // block, advance, (first.astype(jnp.float32), step.astype(jnp.float32))
        )

    @pl.loop(0, slabs)
    def _(s):
        fetch(s).wait()
        at = pl.ds(pl.multiple_of(s * slab, slab), slab)
        high, low = split(stage[s])
        high_q[:, at] = high
        low_q[:, at] = low

    def make(t, high, low):
        s = lax.rem(t, slabs)
        at = pl.ds(pl.multiple_of(lax.div(t, slabs) * chunk, chunk), chunk)
        blank = jnp.zeros((32, chunk), jnp.bfloat16)
        for b in range(slab_blocks):
            coef = jnp.concatenate([cross[:, at], vary[s * slab_blocks + b, :, at], blank], axis=0)
            x = mix(feat_ref[...], coef) * (1.0 / modulus)
            top, rest = split(x - jnp.round(x))
            high[pl.ds(b * block, block), :] = top
            low[pl.ds(b * block, block), :] = rest

    def use(t, high, low):
        s = lax.rem(t, slabs)
        at = pl.ds(pl.multiple_of(s * slab, slab), slab)
        qh = high_q[:, at]
        wh = high[...]
        total[...] += mix(qh, wh) + mix(low_q[:, at], wh) + mix(qh, low[...])

    def cols(n):
        return pl.ds(n * chunk, chunk)

    def pair_copy(n):
        return pltpu.make_async_remote_copy(
            src_ref=part.at[pl.ds(pl.multiple_of((1 - core) * half, half), half), cols(n)],
            dst_ref=pair_in.at[n], send_sem=pair_sem.at[0, n], recv_sem=pair_sem.at[1, n],
            device_id={"param": sibling}, device_id_type=MESH,
        )

    def ring_copy(n, o):
        to = partner(o)
        return pltpu.make_async_remote_copy(
            src_ref=part.at[pl.ds(pl.multiple_of(core * half + to * own, own), own), cols(n)],
            dst_ref=ring_in.at[n, o - 1],
            send_sem=ring_sem.at[0, n, o - 1], recv_sem=ring_sem.at[1, n, o - 1],
            device_id={"param": to * 2 + core}, device_id_type=MESH,
        )

    own_rows = pl.ds(pl.multiple_of(core * half + chip * own, own), own)
    half_rows = pl.ds(pl.multiple_of(core * half, half), half)

    def gather_copy(n, o):
        return pltpu.make_async_remote_copy(
            src_ref=proj.at[own_rows, cols(n)], dst_ref=proj.at[own_rows, cols(n)],
            send_sem=gather_sem.at[0, n, o - 1], recv_sem=gather_sem.at[1, n, o - 1],
            device_id={"param": partner(o) * 2 + core}, device_id_type=MESH,
        )

    def back_copy(n):
        return pltpu.make_async_remote_copy(
            src_ref=proj.at[half_rows, cols(n)], dst_ref=proj.at[half_rows, cols(n)],
            send_sem=back_sem.at[0, n], recv_sem=back_sem.at[1, n],
            device_id={"param": sibling}, device_id_type=MESH,
        )

    def begin(n):
        column = here * width + n * chunk + lax.broadcasted_iota(jnp.int32, (1, chunk), 1)
        gain = jnp.sqrt(1.0 + column.astype(jnp.float32) * (2.0 / width_total)) * scale
        part[:, cols(n)] = total[...] * gain
        pair_copy(n).start()

    def spread(n):
        pair_copy(n).wait_recv()
        part[half_rows, cols(n)] += pair_in[n]
        for o in range(1, chips):
            ring_copy(n, o).start()

    def join(n):
        value = part[own_rows, cols(n)]
        for o in range(1, chips):
            ring_copy(n, o).wait_recv()
            value += ring_in[n, o - 1]
        proj[own_rows, cols(n)] = value
        for o in range(1, chips):
            gather_copy(n, o).start()

    def hand_back(n):
        for o in range(1, chips):
            gather_copy(n, o).wait_recv()
        back_copy(n).start()

    def score(n):
        back_copy(n).wait_recv()
        value = proj[:, cols(n)]
        if n == 0:
            fetch_store.wait()
        high, low = split(value)
        squares = jnp.sum(value * value, axis=1, keepdims=True)
        squares = jnp.broadcast_to(squares, (queries, 128))
        column_sum[...] = squares if n == 0 else column_sum[...] + squares
        tile = min(store_rows, 256)
        for r in range(store_rows // tile):
            at = pl.ds(r * tile, tile)
            sh, sl = split(store[at, cols(n)])
            term = mix_rows(high, sh) + mix_rows(low, sh) + mix_rows(high, sl)
            raw[:, at] = term if n == 0 else raw[:, at] + term

    make(0, high_a, low_a)
    pl.semaphore_wait(barrier, n_param // 2 + n_proj - 1)

    for n in range(chunks):
        total[...] = jnp.zeros_like(total)
        for pair in range(slabs // 2):
            t = n * slabs + pair * 2
            make(t + 1, high_b, low_b)
            use(t, high_a, low_a)
            if t + 2 < chunks * slabs:
                make(t + 2, high_a, low_a)
            use(t + 1, high_b, low_b)
            if n > 0:
                if pair == 0:
                    spread(n - 1)
                if pair == slabs // 4:
                    join(n - 1)
                if pair == slabs // 2 - 1:
                    hand_back(n - 1)
            if n > 1 and pair == 1:
                score(n - 2)
        begin(n)
    last = chunks - 1
    spread(last)
    if chunks > 1:
        score(last - 1)
    join(last)
    hand_back(last)
    score(last)

    square_out[...] = column_sum[...].T[:8, :]

    def square_copy(o):
        return pltpu.make_async_remote_copy(
            src_ref=square_out, dst_ref=square_in.at[o - 1],
            send_sem=square_sem.at[0, o - 1], recv_sem=square_sem.at[1, o - 1],
            device_id={"proj": lax.rem(here + o, n_proj)}, device_id_type=MESH,
        )

    for o in range(1, n_proj):
        square_copy(o).start()

    def line_rows(goal, p):
        return pl.ds(pl.multiple_of(goal * share + p * piece, piece), piece)

    def line_copy(way, goal, p):
        return pltpu.make_async_remote_copy(
            src_ref=raw.at[line_rows(goal, p), :], dst_ref=line_in.at[way, goal, p],
            send_sem=line_sem.at[0, way, goal, p], recv_sem=line_sem.at[1, way, goal, p],
            device_id={"proj": lax.rem(here + 1 - 2 * way + n_proj, n_proj)}, device_id_type=MESH,
        )

    def arrived(way, goal, p):
        line_copy(way, goal, p).wait_recv()
        raw[line_rows(goal, p), :] += line_in[way, goal, p]

    late = (here >= (n_proj + 1) // 2).astype(jnp.int32)

    def moves(k, way):
        goal = (1 - way) * (n_proj - 1 - k) + way * k
        ahead = (goal - here) * (1 - 2 * way)
        behind = (1 - way) * here + way * (n_proj - 1 - here)
        return goal, ahead, behind

    for k in range(n_proj - 1):
        for p in range(pieces):
            for order in range(2):
                way = late + order - 2 * late * order
                goal, ahead, behind = moves(k, way)

                @pl.when(ahead > 0)
                def _():
                    @pl.when(behind > 0)
                    def _():
                        arrived(way, goal, p)

                    line_copy(way, goal, p).start()

    whole = column_sum[...].T[:8, :]
    for o in range(1, n_proj):
        square_copy(o).wait_recv()
        whole += square_in[o - 1]
    inverse = lax.rsqrt(whole * (1.0 / width_total) + epsilon) * (1.0 / math.sqrt(width_total))
    column_sum[...] = jnp.broadcast_to(inverse[:1, :], (128, queries)).T
    for p in range(pieces):
        @pl.when(here > 0)
        def _():
            arrived(0, here, p)

        @pl.when(here < n_proj - 1)
        def _():
            arrived(1, here, p)

        rows = line_rows(here, p)
        factor = column_sum[rows, :][:, :1]
        out_ref[pl.ds(p * piece, piece), :] = jnp.tanh(raw[rows, :] * factor)

    for n in range(chunks):
        pair_copy(n).wait_send()
        back_copy(n).wait_send()
        for o in range(1, chips):
            ring_copy(n, o).wait_send()
            gather_copy(n, o).wait_send()
    for o in range(1, n_proj):
        square_copy(o).wait_send()
    for k in range(n_proj - 1):
        for p in range(pieces):
            for way in range(2):
                goal, ahead, behind = moves(k, way)

                @pl.when(ahead > 0)
                def _():
                    line_copy(way, goal, p).wait_send()


def on_device(query_grads, stored, proj_seed, offsets):
    n_param = lax.axis_size("param")
    n_proj = lax.axis_size("proj")
    queries, coords = query_grads.shape
    store_rows, width = stored.shape
    chips = n_param // 2
    chunks = width // chunk
    slabs = coords // slab
    share = queries // n_proj
    own = queries // n_param
    vmem = pl.BlockSpec(memory_space=pltpu.VMEM)
    smem = pl.BlockSpec(memory_space=pltpu.SMEM)
    hbm = pl.BlockSpec(memory_space=pl.ANY)
    weight = pltpu.VMEM((slab, chunk), jnp.bfloat16)
    dma = pltpu.SemaphoreType.DMA
    return pl.pallas_call(
        functools.partial(kernel, n_param, n_proj),
        out_shape=jax.ShapeDtypeStruct((share, store_rows), jnp.float32),
        in_specs=[smem, smem, vmem, vmem, hbm, hbm],
        out_specs=vmem,
        scratch_shapes=[
            pltpu.VMEM((slabs, queries, slab), jnp.float32),
            pltpu.VMEM((store_rows, width), jnp.float32),
            pltpu.VMEM((queries, coords), jnp.bfloat16),
            pltpu.VMEM((queries, coords), jnp.bfloat16),
            pltpu.VMEM((64, width), jnp.bfloat16),
            pltpu.VMEM((coords // block, 32, width), jnp.bfloat16),
            weight, weight, weight, weight,
            pltpu.VMEM((queries, chunk), jnp.float32),
            pltpu.VMEM((queries, width), jnp.float32),
            pltpu.VMEM((chunks, queries // 2, chunk), jnp.float32),
            pltpu.VMEM((chunks, chips - 1, own, chunk), jnp.float32),
            pltpu.VMEM((queries, width), jnp.float32),
            pltpu.VMEM((queries, store_rows), jnp.float32),
            pltpu.VMEM((8, queries), jnp.float32),
            pltpu.VMEM((n_proj - 1, 8, queries), jnp.float32),
            pltpu.VMEM((queries, 128), jnp.float32),
            pltpu.VMEM((2, n_proj, pieces, share // pieces, store_rows), jnp.float32),
            dma((slabs,)),
            dma,
            dma((2, chunks)),
            dma((2, chunks, chips - 1)),
            dma((2, chunks, chips - 1)),
            dma((2, chunks)),
            dma((2, n_proj - 1)),
            dma((2, 2, n_proj, pieces)),
        ],
        compiler_params=pltpu.CompilerParams(
            collective_id=0, has_side_effects=True, vmem_limit_bytes=58 * 1024 * 1024
        ),
        name="attribution",
    )(offsets, proj_seed, bit_features(), pair_weights(), query_grads, stored)


def solution(mesh):
    placed = (P(None, "param"), P("param", "proj"), P(), P("param"))
    return jax.shard_map(
        on_device, mesh=mesh, in_specs=placed, out_specs=P("proj", "param"), check_vma=False
    )
```

time: 236 us -> 79.1 us (0.34)
  the two profiles are of different devices: /device:TPU:0 before, /device:TPU:8 now
where the time goes in v2:
time: 79.1 us; the launch traced here: 78.9 us
  Pallas kernels  76.6 us (97%)
  local copies, waits for them, and re-layouts  1.67 us (2%)
    pallas_call x1, Pallas kernels, on_device(): pl.pallas_call(functools.partial(kernel, n_param, n_proj), out_shape=jax....  76.6 us
    unnamed x1, local copies, waits for them, and re-layouts  1.67 us

profile of v2, /device:TPU:8, one launch (start us, length us, event | category | flops | bytes accessed | tf_op | source)
XLA Modules:
  0.0 78.9 jit_solution(17824938684075438383)
XLA Ops:
  0.7 76.6 %attribution.1 = f32[64,1024]{1,0:T(8,128)} custom-call(s32[1]{0:T(128)S(6)} %copy.8.offset_ref, s32[2]{0:T(128)} %seed_ref.1, bf16[256,128]{1,0:T(8,128)(2,1)} %constant.4.clone.feat_ref, s32[32,128]{1,0:T(8,128)} %constant.5.clone.weight_ref, f32[256,8192]{1,0:T(8,128)} %grads_ref.1, f32[1024,1024]{1,0:T(8,128)} %stored_ref.1), custom_call_target="tpu_custom_call" | custom-call | tf_op jit(solution)/shard_map/attribution/pallas_call | solution.py:388
  77.2 1.7 %copy.9 = f32[64,1024]{1,0:T(8,128)} copy(f32[64,1024]{1,0:T(8,128)} %attribution.1) | data formatting | bytes 524288
